TPU v7x, 512 devices: a whole 4x4x16 slice. The times are simulated.
512 devices in a mesh: gx: 32 (over y, x, core), gy: 16 (over z).
Axes of the slice: x: 4, y: 4, z: 16, core: 2. Of those that a mesh axis runs over, the one named last changes fastest.
Arguments:
- field: float32 [1024, 512, 384], P('gx', 'gy'), may hold values from -6 to 6
- vertical: float32 [3, 6, 64, 64], replicated, may hold values from -0.75 to 0.75
- horiz_kernel: float32 [3, 2, 6, 9], replicated, may hold values from 0.05 to 1
- gen_weight: float32 [3, 6], replicated, may hold values from 0.3 to 1.5
Outputs:
- covaried: float32 [1024, 512, 384], P('gx', 'gy')
All inputs are finite; a program needn't handle non-finite values.
Results may differ from a plain program's by a relative error of at most 0.0001.
Values sent between devices are 32-bit elements; how exact they have to be, the bound alone decides.
A program may use at most 64 MiB of HBM per device.

v0:
```python
import jax
import jax.numpy as jnp
from jax import lax
from jax.sharding import PartitionSpec as P

GENS = 2
HALF = 4


def extended(cells, sides, width):
    for axis, dim in sides:
        count = lax.axis_size(axis)
        ends = count - 1
        head = lax.slice_in_dim(cells, 0, width, axis=dim)
        tail = lax.slice_in_dim(cells, cells.shape[dim] - width, cells.shape[dim], axis=dim)
        cells = jnp.concatenate(
            [
                lax.ppermute(tail, axis, [(i, (i + 1) % count) for i in range(ends)]),
                cells,
                lax.ppermute(head, axis, [((i + 1) % count, i) for i in range(ends)]),
            ],
            axis=dim,
        )
    return cells


def taps_apply(padded, kvec, axis, count):
    total = kvec[0] * lax.slice_in_dim(padded, 0, count, axis=axis)
    for step in range(1, 2 * HALF + 1):
        total = total + kvec[step] * lax.slice_in_dim(padded, step, step + count, axis=axis)
    return total


def coarsen(grid):
    nrow, ncol, nlev = grid.shape
    return grid.reshape(nrow // 2, 2, ncol // 2, 2, nlev).mean(axis=(1, 3))


def refine(grid):
    return jnp.repeat(jnp.repeat(grid, 2, axis=0), 2, axis=1)


def vertical_mix(along_y, matrices):
    nrow, ncol, nlev = along_y.shape
    nvar = matrices.shape[0]
    levels = matrices.shape[1]
    split = along_y.reshape(nrow, ncol, nvar, levels)
    mixed = jnp.einsum("abvz,vzw->abvw", split, matrices, precision=lax.Precision.HIGHEST)
    return mixed.reshape(nrow, ncol, nlev)


def filter_level(current, kx_vec, ky_vec, matrices):
    nrow, ncol, nlev = current.shape
    padded = extended(current, (("gx", 0),), HALF)
    along_x = taps_apply(padded, kx_vec, 0, nrow)
    widened = extended(along_x, (("gy", 1),), HALF)
    along_y = taps_apply(widened, ky_vec, 1, ncol)
    return vertical_mix(along_y, matrices)


def body(field, vertical, horiz_kernel, gen_weight):
    levels = vertical.shape[2]
    norms = horiz_kernel / jnp.sum(horiz_kernel, axis=-1, keepdims=True)
    tiles = [field]
    for level in range(1, GENS + 1):
        tiles.append(coarsen(tiles[-1]))
    kx_list = [jnp.repeat(norms[level, 0], levels, axis=0).T for level in range(GENS + 1)]
    ky_list = [jnp.repeat(norms[level, 1], levels, axis=0).T for level in range(GENS + 1)]
    filtered = []
    for level in range(GENS + 1):
        filtered.append(filter_level(tiles[level], kx_list[level], ky_list[level], vertical[level]))
    total = jnp.repeat(gen_weight[GENS], levels) * filtered[GENS]
    for level in range(GENS - 1, -1, -1):
        total = jnp.repeat(gen_weight[level], levels) * filtered[level] + refine(total)
    return total


def solution(mesh):
    in_specs = (P("gx", "gy", None), P(), P(), P())
    out_specs = P("gx", "gy", None)
    return jax.shard_map(body, mesh=mesh, in_specs=in_specs, out_specs=out_specs, check_vma=False)
```

profile of v0, /device:TPU:400, one launch (start us, length us, event | category | flops | bytes accessed | tf_op | source)
XLA Modules:
  0.0 88.3 jit_solution(3766719444492590720)
XLA Ops:
  1.1 1.9 %collective-permute-start = (f32[4,32,384]{2,1,0:T(8,128)S(1)}, f32[4,32,384]{2,1,0:T(8,128)S(1)}, u32[]{:S(2)}, u32[]{:S(2)}) collective-permute-start(f32[4,32,384]{2,1,0:T(8,128)S(1)} %get-tuple-element.63), channel_id=1, source_target_pairs={{0,16},{16,32},{32,48},{48,64},{64,80},{80,96},{96,112},{112,128},... | collective-permute-start | bytes 589832 | tf_op jit(solution)/shard_map/ppermute | solution.py:18
  3.0 5.8 %collective-permute-start.1 = (f32[4,32,384]{2,1,0:T(8,128)S(1)}, f32[4,32,384]{2,1,0:T(8,128)S(1)}, u32[]{:S(2)}, u32[]{:S(2)}) collective-permute-start(f32[4,32,384]{2,1,0:T(8,128)S(1)} %get-tuple-element.64), channel_id=1, source_target_pairs={{16,0},{32,16},{48,32},{64,48},{80,64},{96,80},{112,96},{128,112},... | collective-permute-start | bytes 589832 | tf_op jit(solution)/shard_map/ppermute | solution.py:20
  8.7 2.2 %reshape.123 = f32[16,2,16,2,384]{4,3,2,1,0:T(2,128)S(1)} reshape(f32[32,32,384]{2,1,0:T(8,128)} %param.4) | data formatting | bytes 3145728 | tf_op jit(solution)/shard_map/reshape | solution.py:36
  11.0 1.2 %reduce_sum.28 = f32[16,16,384]{2,1,0:T(8,128)S(1)} reduce(f32[16,2,16,2,384]{4,3,2,1,0:T(2,128)S(1)} %reshape.123, f32[]{:T(128)} %constant.2.clone.1), dimensions={1,3}, to_apply=%region_1.0 | reduce | flops 294912 | bytes 1966084 | tf_op jit(solution)/shard_map/reduce_sum | solution.py:36
  12.2 1.9 %collective-permute-start.4 = (f32[4,16,384]{2,1,0:T(8,128)S(1)}, f32[4,16,384]{2,1,0:T(8,128)S(1)}, u32[]{:S(2)}, u32[]{:S(2)}) collective-permute-start(f32[4,16,384]{2,1,0:T(8,128)S(1)} %get-tuple-element.67), channel_id=1, source_target_pairs={{0,16},{16,32},{32,48},{48,64},{64,80},{80,96},{96,112},{112,128},... | collective-permute-start | bytes 294920 | tf_op jit(solution)/shard_map/ppermute | solution.py:18
  14.7 1.9 %collective-permute-start.8 = (f32[4,8,384]{2,1,0:T(8,128)S(1)}, f32[4,8,384]{2,1,0:T(8,128)S(1)}, u32[]{:S(2)}, u32[]{:S(2)}) collective-permute-start(f32[4,8,384]{2,1,0:T(8,128)S(1)} %get-tuple-element.71), channel_id=1, source_target_pairs={{0,16},{16,32},{32,48},{48,64},{64,80},{80,96},{96,112},{112,128},... | collective-permute-start | bytes 147464 | tf_op jit(solution)/shard_map/ppermute | solution.py:18
  16.6 5.8 %collective-permute-start.9 = (f32[4,8,384]{2,1,0:T(8,128)S(1)}, f32[4,8,384]{2,1,0:T(8,128)S(1)}, u32[]{:S(2)}, u32[]{:S(2)}) collective-permute-start(f32[4,8,384]{2,1,0:T(8,128)S(1)} %get-tuple-element.72), channel_id=1, source_target_pairs={{16,0},{32,16},{48,32},{64,48},{80,64},{96,80},{112,96},{128,112},... | collective-permute-start | bytes 147464 | tf_op jit(solution)/shard_map/ppermute | solution.py:20
  28.5 2.4 %collective-permute-start.5 = (f32[4,16,384]{2,1,0:T(8,128)S(1)}, f32[4,16,384]{2,1,0:T(8,128)S(1)}, u32[]{:S(2)}, u32[]{:S(2)}) collective-permute-start(f32[4,16,384]{2,1,0:T(8,128)S(1)} %get-tuple-element.68), channel_id=1, source_target_pairs={{16,0},{32,16},{48,32},{64,48},{80,64},{96,80},{112,96},{128,112},... | collective-permute-start | bytes 294920 | tf_op jit(solution)/shard_map/ppermute | solution.py:20
  31.0 2.9 %collective-permute-start.10 = (f32[8,4,384]{2,1,0:T(4,128)S(1)}, f32[8,4,384]{2,1,0:T(4,128)S(1)}, u32[]{:S(2)}, u32[]{:S(2)}) collective-permute-start(f32[8,4,384]{2,1,0:T(4,128)S(1)} %get-tuple-element.69), channel_id=1, source_target_pairs={{0,1},{1,2},{2,3},{3,4},{4,5},{5,6},{6,7},{7,8},{8,9},{9,10},{10,1... | collective-permute-start | bytes 147464 | tf_op jit(solution)/shard_map/ppermute | solution.py:18
  34.0 4.1 %collective-permute-start.11 = (f32[8,4,384]{2,1,0:T(4,128)S(1)}, f32[8,4,384]{2,1,0:T(4,128)S(1)}, u32[]{:S(2)}, u32[]{:S(2)}) collective-permute-start(f32[8,4,384]{2,1,0:T(4,128)S(1)} %get-tuple-element.70), channel_id=1, source_target_pairs={{1,0},{2,1},{3,2},{4,3},{5,4},{6,5},{7,6},{8,7},{9,8},{10,9},{11,1... | collective-permute-start | bytes 147464 | tf_op jit(solution)/shard_map/ppermute | solution.py:20
  39.1 1.9 %collective-permute-start.6 = (f32[16,4,384]{2,1,0:T(4,128)}, f32[16,4,384]{2,1,0:T(4,128)}, u32[]{:S(2)}, u32[]{:S(2)}) collective-permute-start(f32[16,4,384]{2,1,0:T(4,128)} %get-tuple-element.65), channel_id=1, source_target_pairs={{0,1},{1,2},{2,3},{3,4},{4,5},{5,6},{6,7},{7,8},{8,9},{9,10},{10,1... | collective-permute-start | bytes 294920 | tf_op jit(solution)/shard_map/ppermute | solution.py:18
  41.0 5.1 %collective-permute-start.7 = (f32[16,4,384]{2,1,0:T(4,128)}, f32[16,4,384]{2,1,0:T(4,128)}, u32[]{:S(2)}, u32[]{:S(2)}) collective-permute-start(f32[16,4,384]{2,1,0:T(4,128)} %get-tuple-element.66), channel_id=1, source_target_pairs={{1,0},{2,1},{3,2},{4,3},{5,4},{6,5},{7,6},{8,7},{9,8},{10,9},{11,1... | collective-permute-start | bytes 294920 | tf_op jit(solution)/shard_map/ppermute | solution.py:20
  46.5 1.3 %convolution_bitcast_fusion.1 = f32[8,8,6,64]{3,1,0,2:T(8,128)S(1)} fusion(f32[8,8,6,64]{3,2,1,0:T(8,128)S(1)} %reshape.128, f32[3,6,64,64]{3,2,1,0:T(8,128)} %param.5), kind=kOutput, calls=%fused_computation.57 | convolution fusion | flops 18874368 | bytes 393216 | tf_op jit(solution)/shard_map/abvz,vzw->abvw/dot_general | solution.py:48
  51.7 1.9 %collective-permute-start.2 = (f32[32,4,384]{2,1,0:T(4,128)}, f32[32,4,384]{2,1,0:T(4,128)}, u32[]{:S(2)}, u32[]{:S(2)}) collective-permute-start(f32[32,4,384]{2,1,0:T(4,128)} %get-tuple-element.59), channel_id=1, source_target_pairs={{0,1},{1,2},{2,3},{3,4},{4,5},{5,6},{6,7},{7,8},{8,9},{9,10},{10,1... | collective-permute-start | bytes 589832 | tf_op jit(solution)/shard_map/ppermute | solution.py:18
  53.6 5.3 %collective-permute-start.3 = (f32[32,4,384]{2,1,0:T(4,128)}, f32[32,4,384]{2,1,0:T(4,128)}, u32[]{:S(2)}, u32[]{:S(2)}) collective-permute-start(f32[32,4,384]{2,1,0:T(4,128)} %get-tuple-element.60), channel_id=1, source_target_pairs={{1,0},{2,1},{3,2},{4,3},{5,4},{6,5},{7,6},{8,7},{9,8},{10,9},{11,1... | collective-permute-start | bytes 589832 | tf_op jit(solution)/shard_map/ppermute | solution.py:20
  59.1 1.9 %fusion.59 = f32[16,16,384]{2,1,0:T(8,128)S(1)} fusion(f32[16,16,384]{2,1,0:T(8,128)S(1)} %fusion.39, f32[16,4,384]{2,1,0:T(4,128)} %collective-permute-done.7, f32[16,4,384]{2,1,0:T(4,128)} %collective-permute-done.6, f32[384]{0:T(512)S(1)} %copy-done.20, f32[384]{0:T(512)S(1)} %copy-done.21, f32[384]{0:T(512)S(1)} %copy-done.22, f32[384]{0:T(512)S(1)} %copy-done.23, ...), kind=kLoop, calls=%fused_computation.106 | loop fusion | flops 2457600 | bytes 996864 | tf_op jit(solution)/shard_map/add | solution.py:30
  61.2 1.8 %convolution_bitcast_fusion = f32[16,16,6,64]{3,1,0,2:T(8,128)S(1)} fusion(f32[16,16,6,64]{3,2,1,0:T(8,128)S(1)} %reshape.124, f32[3,6,64,64]{3,2,1,0:T(8,128)} %param.5), kind=kOutput, calls=%fused_computation.56 | convolution fusion | flops 75497472 | bytes 983040 | tf_op jit(solution)/shard_map/abvz,vzw->abvw/dot_general | solution.py:48
  65.0 2.2 %reshape.133 = f32[32,32,384]{2,1,0:T(8,128)} reshape(f32[32,16,2,384]{3,2,1,0:T(2,128)S(1)} %broadcast_in_dim.52) | data formatting | bytes 3145728 | tf_op jit(solution)/shard_map/reshape | solution.py:40
  67.3 3.8 %fusion.8 = f32[32,32,384]{2,1,0:T(8,128)S(1)} fusion(f32[32,32,384]{2,1,0:T(8,128)S(1)} %fusion.27, f32[32,4,384]{2,1,0:T(4,128)} %collective-permute-done.3, f32[32,4,384]{2,1,0:T(4,128)} %collective-permute-done.2, f32[384]{0:T(512)S(1)} %get-tuple-element.6, f32[384]{0:T(512)S(1)} %get-tuple-element.7, f32[384]{0:T(512)S(1)} %get-tuple-element.8, ...), kind=kLoop, calls=%fused_computation.18 | loop fusion | flops 9830400 | bytes 3552768 | tf_op jit(solution)/shard_map/add | solution.py:30
  71.1 2.4 %reshape.119 = f32[32,32,6,64]{3,2,1,0:T(8,128)} reshape(f32[32,32,384]{2,1,0:T(8,128)S(1)} %fusion.8) | data formatting | bytes 3145728 | tf_op jit(solution)/shard_map/reshape | solution.py:47
  73.4 5.3 %fusion.2 = f32[32,32,6,64]{3,1,0,2:T(8,128)S(1)} fusion(f32[32,32,6,64]{3,2,1,0:T(8,128)} %reshape.119, f32[3,6,64,64]{3,2,1,0:T(8,128)} %param.5), kind=kOutput, calls=%fused_computation.14 | convolution fusion | flops 301989888 | bytes 5963776 | tf_op jit(solution)/shard_map/abvz,vzw->abvw/dot_general | solution.py:48
  78.8 4.7 %copy.25 = f32[32,32,6,64]{3,2,1,0:T(8,128)} copy(f32[32,32,6,64]{3,1,0,2:T(8,128)S(1)} %fusion.2) | data formatting | bytes 3145728 | tf_op jit(solution)/shard_map/abvz,vzw->abvw/transpose | solution.py:48
  83.4 3.4 %reshape.120 = f32[32,32,384]{2,1,0:T(8,128)S(1)} reshape(f32[32,32,6,64]{3,2,1,0:T(8,128)} %copy.25) | data formatting | bytes 3145728 | tf_op jit(solution)/shard_map/reshape | solution.py:49
  86.9 1.4 %multiply_add_fusion = f32[32,32,384]{2,1,0:T(8,128)} fusion(f32[32,32,384]{2,1,0:T(8,128)S(1)} %copy-done.1, f32[32,32,384]{2,1,0:T(8,128)S(1)} %reshape.120, f32[384]{0:T(512)S(1)} %copy-done.18), kind=kLoop, calls=%fused_computation.55 | loop fusion | flops 786432 | bytes 4720128 | tf_op jit(solution)/shard_map/add | solution.py:74
  (139 shorter events, 15.0 us)
Async XLA Ops:
  1.1 48.1 %collective-permute-start = (f32[4,32,384]{2,1,0:T(8,128)S(1)}, f32[4,32,384]{2,1,0:T(8,128)S(1)}, u32[]{:S(2)}, u32[]{:S(2)}) collective-permute-start(f32[4,32,384]{2,1,0:T(8,128)S(1)} %get-tuple-element.63), channel_id=1, source_target_pairs={{0,16},{16,32},{32,48},{48,64},{64,80},{80,96},{96,112},{112,128},... | collective-permute-start | bytes 589832 | tf_op jit(solution)/shard_map/ppermute | solution.py:18
  3.0 46.7 %collective-permute-start.1 = (f32[4,32,384]{2,1,0:T(8,128)S(1)}, f32[4,32,384]{2,1,0:T(8,128)S(1)}, u32[]{:S(2)}, u32[]{:S(2)}) collective-permute-start(f32[4,32,384]{2,1,0:T(8,128)S(1)} %get-tuple-element.64), channel_id=1, source_target_pairs={{16,0},{32,16},{48,32},{64,48},{80,64},{96,80},{112,96},{128,112},... | collective-permute-start | bytes 589832 | tf_op jit(solution)/shard_map/ppermute | solution.py:20
  12.2 10.2 %copy-start.3 = (f32[3,2,6,9]{3,1,2,0:T(2,128)S(1)}, f32[3,2,6,9]{3,1,2,0:T(2,128)}, u32[]{:S(2)}) copy-start(f32[3,2,6,9]{3,1,2,0:T(2,128)} %param.6) | copy-start | bytes 3892
  12.2 14.1 %copy-start.30 = (f32[3,6]{1,0:T(4,128)S(1)}, f32[3,6]{1,0:T(4,128)}, u32[]{:S(2)}) copy-start(f32[3,6]{1,0:T(4,128)} %param.7) | copy-start | bytes 220
  12.2 21.7 %collective-permute-start.4 = (f32[4,16,384]{2,1,0:T(8,128)S(1)}, f32[4,16,384]{2,1,0:T(8,128)S(1)}, u32[]{:S(2)}, u32[]{:S(2)}) collective-permute-start(f32[4,16,384]{2,1,0:T(8,128)S(1)} %get-tuple-element.67), channel_id=1, source_target_pairs={{0,16},{16,32},{32,48},{48,64},{64,80},{80,96},{96,112},{112,128},... | collective-permute-start | bytes 294920 | tf_op jit(solution)/shard_map/ppermute | solution.py:18
  14.7 13.8 %collective-permute-start.8 = (f32[4,8,384]{2,1,0:T(8,128)S(1)}, f32[4,8,384]{2,1,0:T(8,128)S(1)}, u32[]{:S(2)}, u32[]{:S(2)}) collective-permute-start(f32[4,8,384]{2,1,0:T(8,128)S(1)} %get-tuple-element.71), channel_id=1, source_target_pairs={{0,16},{16,32},{32,48},{48,64},{64,80},{80,96},{96,112},{112,128},... | collective-permute-start | bytes 147464 | tf_op jit(solution)/shard_map/ppermute | solution.py:18
  16.6 14.3 %collective-permute-start.9 = (f32[4,8,384]{2,1,0:T(8,128)S(1)}, f32[4,8,384]{2,1,0:T(8,128)S(1)}, u32[]{:S(2)}, u32[]{:S(2)}) collective-permute-start(f32[4,8,384]{2,1,0:T(8,128)S(1)} %get-tuple-element.72), channel_id=1, source_target_pairs={{16,0},{32,16},{48,32},{64,48},{80,64},{96,80},{112,96},{128,112},... | collective-permute-start | bytes 147464 | tf_op jit(solution)/shard_map/ppermute | solution.py:20
  28.5 9.6 %collective-permute-start.5 = (f32[4,16,384]{2,1,0:T(8,128)S(1)}, f32[4,16,384]{2,1,0:T(8,128)S(1)}, u32[]{:S(2)}, u32[]{:S(2)}) collective-permute-start(f32[4,16,384]{2,1,0:T(8,128)S(1)} %get-tuple-element.68), channel_id=1, source_target_pairs={{16,0},{32,16},{48,32},{64,48},{80,64},{96,80},{112,96},{128,112},... | collective-permute-start | bytes 294920 | tf_op jit(solution)/shard_map/ppermute | solution.py:20
  31.0 10.0 %collective-permute-start.10 = (f32[8,4,384]{2,1,0:T(4,128)S(1)}, f32[8,4,384]{2,1,0:T(4,128)S(1)}, u32[]{:S(2)}, u32[]{:S(2)}) collective-permute-start(f32[8,4,384]{2,1,0:T(4,128)S(1)} %get-tuple-element.69), channel_id=1, source_target_pairs={{0,1},{1,2},{2,3},{3,4},{4,5},{5,6},{6,7},{7,8},{8,9},{9,10},{10,1... | collective-permute-start | bytes 147464 | tf_op jit(solution)/shard_map/ppermute | solution.py:18
  34.0 12.2 %collective-permute-start.11 = (f32[8,4,384]{2,1,0:T(4,128)S(1)}, f32[8,4,384]{2,1,0:T(4,128)S(1)}, u32[]{:S(2)}, u32[]{:S(2)}) collective-permute-start(f32[8,4,384]{2,1,0:T(4,128)S(1)} %get-tuple-element.70), channel_id=1, source_target_pairs={{1,0},{2,1},{3,2},{4,3},{5,4},{6,5},{7,6},{8,7},{9,8},{10,9},{11,1... | collective-permute-start | bytes 147464 | tf_op jit(solution)/shard_map/ppermute | solution.py:20
  38.4 9.6 %copy-start.29 = (f32[384]{0:T(512)S(1)}, f32[384]{0:T(512)}, u32[]{:S(2)}) copy-start(f32[384]{0:T(512)} %mul.692) | copy-start | bytes 4612
  39.1 19.9 %collective-permute-start.6 = (f32[16,4,384]{2,1,0:T(4,128)}, f32[16,4,384]{2,1,0:T(4,128)}, u32[]{:S(2)}, u32[]{:S(2)}) collective-permute-start(f32[16,4,384]{2,1,0:T(4,128)} %get-tuple-element.65), channel_id=1, source_target_pairs={{0,1},{1,2},{2,3},{3,4},{4,5},{5,6},{6,7},{7,8},{8,9},{9,10},{10,1... | collective-permute-start | bytes 294920 | tf_op jit(solution)/shard_map/ppermute | solution.py:18
  41.0 18.0 %collective-permute-start.7 = (f32[16,4,384]{2,1,0:T(4,128)}, f32[16,4,384]{2,1,0:T(4,128)}, u32[]{:S(2)}, u32[]{:S(2)}) collective-permute-start(f32[16,4,384]{2,1,0:T(4,128)} %get-tuple-element.66), channel_id=1, source_target_pairs={{1,0},{2,1},{3,2},{4,3},{5,4},{6,5},{7,6},{8,7},{9,8},{10,9},{11,1... | collective-permute-start | bytes 294920 | tf_op jit(solution)/shard_map/ppermute | solution.py:20
  50.0 9.0 %copy-start.19 = (f32[384]{0:T(512)S(1)}, f32[384]{0:T(512)}, u32[]{:S(2)}) copy-start(f32[384]{0:T(512)} %get-tuple-element.23) | copy-start | bytes 4612
  50.0 9.0 %copy-start.20 = (f32[384]{0:T(512)S(1)}, f32[384]{0:T(512)}, u32[]{:S(2)}) copy-start(f32[384]{0:T(512)} %get-tuple-element.24) | copy-start | bytes 4612
  50.0 9.1 %copy-start.21 = (f32[384]{0:T(512)S(1)}, f32[384]{0:T(512)}, u32[]{:S(2)}) copy-start(f32[384]{0:T(512)} %get-tuple-element.25) | copy-start | bytes 4612
  50.0 9.1 %copy-start.22 = (f32[384]{0:T(512)S(1)}, f32[384]{0:T(512)}, u32[]{:S(2)}) copy-start(f32[384]{0:T(512)} %get-tuple-element.26) | copy-start | bytes 4612
  50.0 9.1 %copy-start.23 = (f32[384]{0:T(512)S(1)}, f32[384]{0:T(512)}, u32[]{:S(2)}) copy-start(f32[384]{0:T(512)} %get-tuple-element.27) | copy-start | bytes 4612
  50.0 9.1 %copy-start.24 = (f32[384]{0:T(512)S(1)}, f32[384]{0:T(512)}, u32[]{:S(2)}) copy-start(f32[384]{0:T(512)} %get-tuple-element.28) | copy-start | bytes 4612
  50.0 9.1 %copy-start.25 = (f32[384]{0:T(512)S(1)}, f32[384]{0:T(512)}, u32[]{:S(2)}) copy-start(f32[384]{0:T(512)} %get-tuple-element.29) | copy-start | bytes 4612
  50.0 9.1 %copy-start.26 = (f32[384]{0:T(512)S(1)}, f32[384]{0:T(512)}, u32[]{:S(2)}) copy-start(f32[384]{0:T(512)} %get-tuple-element.30) | copy-start | bytes 4612
  50.0 9.1 %copy-start.27 = (f32[384]{0:T(512)S(1)}, f32[384]{0:T(512)}, u32[]{:S(2)}) copy-start(f32[384]{0:T(512)} %get-tuple-element.31) | copy-start | bytes 4612
  51.7 15.5 %collective-permute-start.2 = (f32[32,4,384]{2,1,0:T(4,128)}, f32[32,4,384]{2,1,0:T(4,128)}, u32[]{:S(2)}, u32[]{:S(2)}) collective-permute-start(f32[32,4,384]{2,1,0:T(4,128)} %get-tuple-element.59), channel_id=1, source_target_pairs={{0,1},{1,2},{2,3},{3,4},{4,5},{5,6},{6,7},{7,8},{8,9},{9,10},{10,1... | collective-permute-start | bytes 589832 | tf_op jit(solution)/shard_map/ppermute | solution.py:18
  53.6 13.6 %collective-permute-start.3 = (f32[32,4,384]{2,1,0:T(4,128)}, f32[32,4,384]{2,1,0:T(4,128)}, u32[]{:S(2)}, u32[]{:S(2)}) collective-permute-start(f32[32,4,384]{2,1,0:T(4,128)} %get-tuple-element.60), channel_id=1, source_target_pairs={{1,0},{2,1},{3,2},{4,3},{5,4},{6,5},{7,6},{8,7},{9,8},{10,9},{11,1... | collective-permute-start | bytes 589832 | tf_op jit(solution)/shard_map/ppermute | solution.py:20
  (19 other events, 27.8 us)
where the time goes:
time: 89 us; the launch traced here: 88.3 us
  starting transfers between devices  41 us (46%)
  local copies, waits for them, and re-layouts  27.9 us (31%)
  other arithmetic  10.2 us (11%)
  matrix products  8.37 us (9%)
    ppermute x6, starting transfers between devices, extended(): lax.ppermute(head, axis, [((i + 1) % count, i) for i in range(ends)])  28.5 us
    ppermute x6, starting transfers between devices, extended(): lax.ppermute(tail, axis, [(i, (i + 1) % count) for i in range(ends)])  12.5 us
    dot_general x3, matrix products, vertical_mix(): jnp.einsum('abvz,vzw->abvw', split, matrices, precision=lax.Precision.HIG...  8.37 us
    add x6, other arithmetic, taps_apply(): total + kvec[step] * lax.slice_in_dim(padded, step, step + count, axis=axis)  7 us
    transpose x3, local copies, waits for them, and re-layouts, vertical_mix(): jnp.einsum('abvz,vzw->abvw', split, matrices, precision=lax.Precision.HIG...  5.26 us
    reshape x3, local copies, waits for them, and re-layouts, vertical_mix(): return mixed.reshape(nrow, ncol, nlev)  3.74 us
    reshape x2, local copies, waits for them, and re-layouts, refine(): return jnp.repeat(jnp.repeat(grid, 2, axis=0), 2, axis=1)  3.24 us
    reshape x3, local copies, waits for them, and re-layouts, vertical_mix(): split = along_y.reshape(nrow, ncol, nvar, levels)  2.71 us
  transfers between devices with their start and end apart: 12, of which 0 were waited for; matrix products, arithmetic and copies ran while one was open for 27% of the time, Pallas kernels for 0%

commit v1 on v0

v1 whole, which is shorter than its diff:
```python
import functools

import jax
import jax.numpy as jnp
from jax import lax
from jax.experimental import pallas as pl
from jax.experimental.pallas import tpu as pltpu
from jax.sharding import PartitionSpec as P

GENS = 3
HALF = 4
TAPS = 9
VARS = 6
LEVELS = 64
LANES = 128
GROUPS = 3
MESH = pl.DeviceIdType.MESH
F32 = jnp.float32
BF16 = jnp.bfloat16


def line_sum(pieces, taps):
    total = taps[0] * pieces[0]
    for step in range(1, TAPS):
        total = total + taps[step] * pieces[step]
    return total


def kernel(nx, ny, field, vertical, horiz, weight, out,
           grid0, grid1, grid2, side0, side1, side2, wide0, wide1, wide2,
           vert, hk, gw, taps, wfull, mats, pair, left0, left1, left2, up1, up2,
           load_sem, send_sem, recv_sem):
    gx, gy = lax.axis_index("gx"), lax.axis_index("gy")
    grids, sides, wides = (grid0, grid1, grid2), (side0, side1, side2), (wide0, wide1, wide2)
    sizes = (32, 16, 8)

    loads = [
        pltpu.make_async_copy(
            field.at[:, :, pl.ds(g * LANES, LANES)], grid0.at[g, pl.ds(HALF, 32)], load_sem.at[g])
        for g in range(GROUPS)
    ]
    for n, (src, dst) in enumerate(((vertical, vert), (horiz, hk), (weight, gw))):
        loads.append(pltpu.make_async_copy(src, dst, load_sem.at[GROUPS + n]))
    for load in loads:
        load.start()

    has = {"xl": gx > 0, "xr": gx < nx - 1, "zl": gy > 0, "zr": gy < ny - 1}
    ids = {"xl": {"gx": gx - 1}, "xr": {"gx": gx + 1}, "zl": {"gy": gy - 1}, "zr": {"gy": gy + 1}}
    back = {"xl": "xr", "xr": "xl", "zl": "zr", "zr": "zl"}

    barrier = pltpu.get_barrier_semaphore()
    for way in has:
        @pl.when(has[way])
        def _(way=way):
            pl.semaphore_signal(barrier, inc=1, device_id=ids[way], device_id_type=MESH)

    for way in has:
        @pl.when(jnp.logical_not(has[way]))
        def _(way=way):
            for grid, side, size in zip(grids, sides, sizes):
                if way == "xl":
                    grid[:, 0:HALF] = jnp.zeros((GROUPS, HALF, size, LANES), F32)
                    side[:, 0:HALF] = jnp.zeros((GROUPS, HALF, 8, LANES), F32)
                elif way == "xr":
                    grid[:, size + HALF:] = jnp.zeros((GROUPS, HALF, size, LANES), F32)
                    side[:, size + HALF:] = jnp.zeros((GROUPS, HALF, 8, LANES), F32)
                else:
                    at = HALF if way == "zl" else 0
                    side[:, HALF:size + HALF, at:at + HALF] = jnp.zeros((GROUPS, size, HALF, LANES), F32)

    copies = {}

    def add(name, way, src, dst):
        slot = len(copies)
        copies[name] = (way, pltpu.make_async_remote_copy(
            src_ref=src, dst_ref=dst, send_sem=send_sem.at[slot], recv_sem=recv_sem.at[slot],
            device_id=ids[way], device_id_type=MESH))

    every = pl.ds(0, GROUPS)
    for level, size in enumerate(sizes):
        grid, side = grids[level], sides[level]
        low, high = pl.ds(HALF, HALF), pl.ds(size, HALF)
        add(("x", level, "xl"), "xl", grid.at[:, low], grid.at[:, pl.ds(size + HALF, HALF)])
        add(("x", level, "xr"), "xr", grid.at[:, high], grid.at[:, pl.ds(0, HALF)])
        add(("c", level, "xl"), "xl", side.at[:, low], side.at[:, pl.ds(size + HALF, HALF)])
        add(("c", level, "xr"), "xr", side.at[:, high], side.at[:, pl.ds(0, HALF)])
        for way, here, there in (("zl", 0, 0), ("zr", size - HALF, HALF)):
            cols, to = pl.ds(here, HALF), pl.ds(there, HALF)
            if level == 2:
                rows = pl.ds(HALF, size)
                add(("z", level, "lo", way), way, grid.at[:, rows, cols], side.at[:, rows, to])
            else:
                add(("z", level, "lo", way), way, grid.at[:, low, cols], side.at[:, low, to])
                add(("z", level, "hi", way), way, grid.at[:, high, cols], side.at[:, high, to])
                rows = pl.ds(2 * HALF, size - 2 * HALF)
                for g in range(GROUPS):
                    add(("z", level, g, way), way, grid.at[g, rows, cols], side.at[g, rows, to])

    def each(names, act):
        by_way = {}
        for name in names:
            by_way.setdefault(name[-1], []).append(name)
        for way, group in by_way.items():
            gate = has[back[way]] if act == "wait_recv" else has[way]

            @pl.when(gate)
            def _(group=group):
                for name in group:
                    getattr(copies[name][1], act)()

    xs, zs = ("xl", "xr"), ("zl", "zr")
    for g in range(GROUPS):
        loads[g].wait()
    pl.semaphore_wait(barrier, sum(flag.astype(jnp.int32) for flag in has.values()))

    first = [("z", 0, end, way) for end in ("lo", "hi") for way in zs] + [("x", 0, way) for way in xs]
    each(first, "start")

    def coarsen(g, carry):
        for fine, coarse, size in ((grid0, grid1, 16), (grid1, grid2, 8)):
            def rows(r, c):
                base = HALF + 2 * r
                pair[r, 0:2 * size] = fine[g, base] + fine[g, base + 1]
                coarse[g, HALF + r] = 0.25 * (
                    pair[r, pl.ds(0, size, stride=2)] + pair[r, pl.ds(1, size, stride=2)])
                return c
            lax.fori_loop(0, size, rows, 0, unroll=True)
        return carry

    lax.fori_loop(0, GROUPS, coarsen, 0)

    second = [("z", 1, "lo", way) for way in zs] + [("z", 1, "hi", way) for way in zs]
    second += [("z", 2, "lo", way) for way in zs]
    second += [("x", level, way) for level in (1, 2) for way in xs]
    each(second, "start")
    third = [("z", level, g, way) for g in range(GROUPS) for level in (0, 1) for way in zs]
    each(third, "start")

    for load in loads[GROUPS:]:
        load.wait()
    lane = lax.broadcasted_iota(jnp.int32, (VARS, GROUPS * LANES), 1)
    row = lax.broadcasted_iota(jnp.int32, (VARS, GROUPS * LANES), 0)
    pick = jnp.where((lane >= row * LEVELS) & (lane < (row + 1) * LEVELS), 1.0, 0.0).astype(F32)
    for level in range(GENS):
        for axis in range(2):
            norm = hk[level, axis] / jnp.sum(hk[level, axis], axis=-1, keepdims=True)
            spread = lax.dot_general(norm, pick, (((0,), (0,)), ((), ())),
                                     precision=lax.Precision.HIGHEST, preferred_element_type=F32)
            for g in range(GROUPS):
                taps[level, axis, g, 0:TAPS] = spread[:, g * LANES:(g + 1) * LANES]
    scale = jnp.dot(gw[...], pick, precision=lax.Precision.HIGHEST, preferred_element_type=F32)
    wfull[...] = jnp.zeros_like(wfull)
    for level in range(GENS):
        for g in range(GROUPS):
            wfull[0:LEVELS, 0:LEVELS] = vert[level, 2 * g]
            wfull[LEVELS:LANES, LEVELS:LANES] = vert[level, 2 * g + 1]
            whole = wfull[...] * scale[level:level + 1, g * LANES:(g + 1) * LANES]
            head = whole.astype(BF16)
            tail = (whole - head.astype(F32)).astype(BF16)
            for at in (0, LANES):
                mats[level, g, at:at + LANES, 0:LANES] = head
                mats[level, g, at:at + LANES, LANES:] = tail

    def taps_of(level, axis, g):
        return [taps[level, axis, g, step:step + 1] for step in range(TAPS)]

    def along_x(source, g, r, cols, ktaps):
        block = source[g, pl.ds(r, 16), cols]
        return line_sum([block[step:step + 8] for step in range(TAPS)], ktaps)

    each([("x", 0, way) for way in xs], "wait_recv")

    def own_x(level, g):
        size = sizes[level]
        ktaps = taps_of(level, 0, g)

        def rows(n, carry):
            r = n * 8
            for t in range(size // 8):
                wides[level][g, pl.ds(r, 8), 8 + 8 * t:16 + 8 * t] = along_x(
                    grids[level], g, r, pl.ds(8 * t, 8), ktaps)
            return carry

        lax.fori_loop(0, size // 8, rows, 0)

    def own0(g, carry):
        own_x(0, g)
        return carry

    lax.fori_loop(0, GROUPS, own0, 0)

    each([("z", level, end, way) for level in (0, 1) for end in ("lo", "hi") for way in zs]
         + [("z", 2, "lo", way) for way in zs], "wait_recv")
    corners = [("c", level, way) for level in range(GENS) for way in xs]
    each(corners, "start")

    each([("x", level, way) for level in (1, 2) for way in xs], "wait_recv")

    def own12(g, carry):
        own_x(1, g)
        own_x(2, g)
        return carry

    lax.fori_loop(0, GROUPS, own12, 0)
    each(corners, "wait_recv")

    for g in range(GROUPS):
        each([("z", level, g, way) for level in (0, 1) for way in zs], "wait_recv")
        for level in (2, 1, 0):
            size, side, wide = sizes[level], sides[level], wides[level]
            left = (left0, left1, left2)[level]
            kx, ky = taps_of(level, 0, g), taps_of(level, 1, g)
            tiles = size // 8

            def rows(n, carry):
                r = n * 8 if isinstance(n, int) else pl.multiple_of(n * 8, 8)
                halo = along_x(side, g, r, pl.ds(0, 8), kx)
                wide[g, pl.ds(r, 8), 0:8] = halo
                wide[g, pl.ds(r, 8), size + 8:size + 16] = halo
                for t in range(tiles):
                    mixed = line_sum(
                        [wide[g, pl.ds(r, 8), 8 * t + HALF + step:8 * t + HALF + step + 8] for step in range(TAPS)],
                        ky).reshape(64, LANES)
                    head = mixed.astype(BF16)
                    tail = (mixed - head.astype(F32)).astype(BF16)
                    at = pl.ds(n * (64 * tiles) + 64 * t, 64)
                    left[at, 0:LANES] = head
                    left[at, LANES:] = tail
                return carry

            lax.fori_loop(0, size // 8, rows, 0)

            def product(n, carry):
                both = jnp.dot(left[pl.ds(n * (64 * tiles), 64 * tiles)], mats[level, g],
                               preferred_element_type=F32)
                total = both[:, 0:LANES] + both[:, LANES:]
                for t in range(tiles):
                    part = total[64 * t:64 * t + 64].reshape(8, 8, LANES)
                    if level < 2:
                        coarse = (up1, up2)[level][pl.ds(n * 4, 4), 8 * t:8 * t + 8]
                        part = part + jnp.broadcast_to(coarse[:, None], (4, 2, 8, LANES)).reshape(8, 8, LANES)
                    if level == 0:
                        out[pl.ds(n * 8, 8), 8 * t:8 * t + 8, g * LANES:(g + 1) * LANES] = part
                    else:
                        finer = (up1, up2)[level - 1]
                        for i in range(8):
                            for odd in range(2):
                                finer[n * 8 + i, pl.ds(16 * t + odd, 8, stride=2)] = part[i]
                return carry

            lax.fori_loop(0, size // 8, product, 0)

    each(list(copies), "wait_send")


def solution(mesh):
    nx, ny = mesh.shape["gx"], mesh.shape["gy"]

    def body(field, vertical, horiz_kernel, gen_weight):
        vmem = pltpu.VMEM
        return pl.pallas_call(
            functools.partial(kernel, nx, ny),
            out_shape=jax.ShapeDtypeStruct(field.shape, F32),
            in_specs=[pl.BlockSpec(memory_space=pltpu.MemorySpace.HBM)] * 4,
            out_specs=pl.BlockSpec(memory_space=pltpu.MemorySpace.VMEM),
            scratch_shapes=[
                vmem((GROUPS, 40, 32, LANES), F32),
                vmem((GROUPS, 24, 16, LANES), F32),
                vmem((GROUPS, 16, 8, LANES), F32),
                vmem((GROUPS, 40, 8, LANES), F32),
                vmem((GROUPS, 24, 8, LANES), F32),
                vmem((GROUPS, 16, 8, LANES), F32),
                vmem((GROUPS, 32, 48, LANES), F32),
                vmem((GROUPS, 16, 32, LANES), F32),
                vmem((GROUPS, 8, 24, LANES), F32),
                vmem(vertical.shape, F32),
                vmem(horiz_kernel.shape, F32),
                vmem(gen_weight.shape, F32),
                vmem((GENS, 2, GROUPS, 16, LANES), F32),
                vmem((LANES, LANES), F32),
                vmem((GENS, GROUPS, 2 * LANES, 2 * LANES), BF16),
                vmem((16, 32, LANES), F32),
                vmem((1024, 2 * LANES), BF16),
                vmem((256, 2 * LANES), BF16),
                vmem((64, 2 * LANES), BF16),
                vmem((16, 32, LANES), F32),
                vmem((8, 16, LANES), F32),
                pltpu.SemaphoreType.DMA((GROUPS + 3,)),
                pltpu.SemaphoreType.DMA((34,)),
                pltpu.SemaphoreType.DMA((34,)),
            ],
            compiler_params=pltpu.CompilerParams(
                collective_id=0, has_side_effects=True, vmem_limit_bytes=40 * 2 ** 20),
        )(field, vertical, horiz_kernel, gen_weight)

    return jax.shard_map(
        body, mesh=mesh, in_specs=(P("gx", "gy", None), P(), P(), P()),
        out_specs=P("gx", "gy", None), check_vma=False)
```

time: 89 us -> 28.8 us (0.32)
  the two profiles are of different devices: /device:TPU:400 before, /device:TPU:1 now
where the time goes in v1:
time: 28.8 us; the launch traced here: 28.5 us
  Pallas kernels  23.5 us (82%)
  local copies, waits for them, and re-layouts  5.02 us (17%)
    pallas_call x1, Pallas kernels, body(): pl.pallas_call(functools.partial(kernel, nx, ny), out_shape=jax.ShapeDtyp...  23.5 us
    unnamed x8, local copies, waits for them, and re-layouts  5.02 us

profile of v1, /device:TPU:1, one launch (start us, length us, event | category | flops | bytes accessed | tf_op | source)
XLA Modules:
  0.0 28.5 jit_solution(3987106080524523077)
XLA Ops:
  0.0 0.7 %copy.5.horiz = f32[3,2,6,9]{3,2,1,0:T(8,128)S(1)} copy(f32[3,2,6,9]{3,1,2,0:T(2,128)} %param.6) | data formatting | bytes 2592 | tf_op args[2]
  0.7 0.0 copy-start
  0.7 1.4 %copy-done = f32[32,32,384]{2,1,0:T(8,128)S(1)} copy-done((f32[32,32,384]{2,1,0:T(8,128)S(1)}, f32[32,32,384]{2,1,0:T(8,128)}, u32[]{:S(2)}) %copy-start) | copy-done | bytes 1572888
  2.1 0.0 copy-start.1
  2.1 1.1 %copy-done.1 = f32[3,6,64,64]{3,2,1,0:T(8,128)S(1)} copy-done((f32[3,6,64,64]{3,2,1,0:T(8,128)S(1)}, f32[3,6,64,64]{3,2,1,0:T(8,128)}, u32[]{:S(2)}) %copy-start.1) | copy-done | bytes 294936
  3.2 0.0 copy-start.2
  3.2 0.7 %copy-done.2 = f32[3,6]{1,0:T(4,128)S(1)} copy-done((f32[3,6]{1,0:T(4,128)S(1)}, f32[3,6]{1,0:T(4,128)}, u32[]{:S(2)}) %copy-start.2) | copy-done | bytes 96
  3.9 23.5 %shard_map.46 = f32[32,32,384]{2,1,0:T(8,128)S(1)} custom-call(f32[32,32,384]{2,1,0:T(8,128)S(1)} %copy-done, f32[3,6,64,64]{3,2,1,0:T(8,128)S(1)} %copy-done.1, f32[3,2,6,9]{3,2,1,0:T(8,128)S(1)} %copy.5.horiz, f32[3,6]{1,0:T(4,128)S(1)} %copy-done.2), custom_call_target="tpu_custom_call" | custom-call | tf_op jit(solution)/shard_map/pallas_call | solution.py:261
  27.3 1.1 %copy.7 = f32[32,32,384]{2,1,0:T(8,128)} copy(f32[32,32,384]{2,1,0:T(8,128)S(1)} %shard_map.46) | data formatting | bytes 3145728
Async XLA Ops:
  0.7 1.4 %copy-start = (f32[32,32,384]{2,1,0:T(8,128)S(1)}, f32[32,32,384]{2,1,0:T(8,128)}, u32[]{:S(2)}) copy-start(f32[32,32,384]{2,1,0:T(8,128)} %field.1) | copy-start | bytes 4718596
  2.1 1.1 %copy-start.1 = (f32[3,6,64,64]{3,2,1,0:T(8,128)S(1)}, f32[3,6,64,64]{3,2,1,0:T(8,128)}, u32[]{:S(2)}) copy-start(f32[3,6,64,64]{3,2,1,0:T(8,128)} %vertical.1) | copy-start | bytes 884740
  3.2 0.7 %copy-start.2 = (f32[3,6]{1,0:T(4,128)S(1)}, f32[3,6]{1,0:T(4,128)}, u32[]{:S(2)}) copy-start(f32[3,6]{1,0:T(4,128)} %weight.1) | copy-start | bytes 220

commit v2 on v0

v2 whole, which is shorter than its diff:
```python
import functools

import jax
import jax.numpy as jnp
from jax import lax
from jax.experimental import pallas as pl
from jax.experimental.pallas import tpu as pltpu
from jax.sharding import PartitionSpec as P

GENS = 3
HALF = 4
TAPS = 9
VARS = 6
LEVELS = 64
LANES = 128
GROUPS = 3
SIZES = (32, 16, 8)
MESH = pl.DeviceIdType.MESH
F32 = jnp.float32
BF16 = jnp.bfloat16

BELOW, LOW, HIGH, MIDDLE, ABOVE, ROWS = 0, 12, 24, 36, 68, 80
UNITS = (
    (0, 12, 36, 40, 44, 48, 52, 56, 24, 68),
    (4, 16, 60, 64, 28, 72),
    (8, 20, 32, 76),
)


def line_sum(pieces, taps):
    total = taps[0] * pieces[0]
    for piece, tap in zip(pieces[1:], taps[1:]):
        total = total + tap * piece
    return total


def split_into(ref, at, values):
    rows = values.shape[0] * values.shape[1]
    flat = values.reshape(rows, LANES)
    head = flat.astype(BF16)
    ref[at:at + rows, 0:LANES] = head
    ref[at:at + rows, LANES:] = (flat - head.astype(F32)).astype(BF16)


def kernel(nx, ny, field, vertical, horiz, weight, out,
           grid0, grid1, grid2, send, halo, wide0a, wide0b, wide1a, wide1b, wide2,
           vert, hk, gw, taps, coef, wfull, mats, pair,
           left0a, left0b, left1a, left1b, left2, twice, left_edge, part1, part2, up1, up2,
           load_sem, send_sem, recv_sem):
    gx, gy = lax.axis_index("gx"), lax.axis_index("gy")
    grids = (grid0, grid1, grid2)

    loads = [
        pltpu.make_async_copy(
            field.at[:, :, pl.ds(g * LANES, LANES)], grid0.at[g, pl.ds(HALF, 32)], load_sem.at[g])
        for g in range(GROUPS)
    ]
    for n, (src, dst) in enumerate(((vertical, vert), (horiz, hk), (weight, gw))):
        loads.append(pltpu.make_async_copy(src, dst, load_sem.at[GROUPS + n]))
    for load in loads:
        load.start()

    has = {"xl": gx > 0, "xr": gx < nx - 1, "zl": gy > 0, "zr": gy < ny - 1}
    ids = {"xl": {"gx": gx - 1}, "xr": {"gx": gx + 1}, "zl": {"gy": gy - 1}, "zr": {"gy": gy + 1}}
    back = {"xl": "xr", "xr": "xl", "zl": "zr", "zr": "zl"}
    xs, zs = ("xl", "xr"), ("zl", "zr")

    barrier = pltpu.get_barrier_semaphore()
    for way in has:
        @pl.when(has[way])
        def _(way=way):
            pl.semaphore_signal(barrier, inc=1, device_id=ids[way], device_id_type=MESH)

    for way in has:
        @pl.when(jnp.logical_not(has[way]))
        def _(way=way):
            if way in xs:
                for grid, size in zip(grids, SIZES):
                    at = 0 if way == "xl" else size + HALF
                    grid[:, at:at + HALF] = jnp.zeros((GROUPS, HALF, size, LANES), F32)
                at = BELOW if way == "xl" else ABOVE
                halo[:, at:at + 12] = jnp.zeros((GROUPS, 12, 8, LANES), F32)
            else:
                at = HALF if way == "zl" else 0
                halo[:, LOW:ABOVE, at:at + HALF] = jnp.zeros((GROUPS, ABOVE - LOW, HALF, LANES), F32)
    for wide, size in ((wide0a, 32), (wide0b, 32), (wide1a, 16), (wide1b, 16), (wide2, 8)):
        wide[:, 0:8] = jnp.zeros((8, 8, LANES), F32)
        wide[:, size + 8:] = jnp.zeros((8, 8, LANES), F32)

    def remote(way, src, dst, slot):
        return pltpu.make_async_remote_copy(
            src_ref=src, dst_ref=dst, send_sem=send_sem.at[slot], recv_sem=recv_sem.at[slot],
            device_id=ids[way], device_id_type=MESH)

    def x_copy(way, level):
        grid, size = grids[level], SIZES[level]
        here, there = (HALF, size + HALF) if way == "xl" else (size, 0)
        return remote(way, grid.at[:, pl.ds(here, HALF)], grid.at[:, pl.ds(there, HALF)],
                      level * 2 + xs.index(way))

    def z_copy(way, part, g):
        start, rows = ((LOW, 24), (MIDDLE, 32))[part]
        cols = pl.ds(zs.index(way) * HALF, HALF)
        return remote(way, send.at[g, pl.ds(start - LOW, rows), cols], halo.at[g, pl.ds(start, rows), cols],
                      6 + part * 6 + zs.index(way) * 3 + g)

    def corner_copy(way, g):
        here, there = (LOW, ABOVE) if way == "xl" else (HIGH, BELOW)
        return remote(way, halo.at[g, pl.ds(here, 12)], halo.at[g, pl.ds(there, 12)],
                      18 + xs.index(way) * 3 + g)

    def start(ways, make):
        for way in ways:
            @pl.when(has[way])
            def _(way=way):
                for copy in make(way):
                    copy.start()

    def arrived(ways, make):
        for way in ways:
            @pl.when(has[back[way]])
            def _(way=way):
                for copy in make(way):
                    copy.wait_recv()

    def sent(ways, make):
        for way in ways:
            @pl.when(has[way])
            def _(way=way):
                for copy in make(way):
                    copy.wait_send()

    lower = lax.broadcasted_iota(jnp.int32, (4, 8, LANES), 1) < HALF

    def prepare(g):
        for fine, coarse, size in ((grid0, grid1, 16), (grid1, grid2, 8)):
            for r in range(size):
                pair[r, 0:2 * size] = fine[g, HALF + 2 * r] + fine[g, HALF + 2 * r + 1]
                coarse[g, HALF + r] = 0.25 * (
                    pair[r, pl.ds(0, size, stride=2)] + pair[r, pl.ds(1, size, stride=2)])
        for level, size in enumerate(SIZES):
            for n, at in enumerate(UNITS[level][1:-1]):
                rows = pl.ds(HALF + 4 * n, 4)
                first, last = grids[level][g, rows, 0:8], grids[level][g, rows, size - 8:size]
                send[g, pl.ds(at - LOW, 4)] = jnp.where(lower, first, last)

    for g in range(GROUPS):
        loads[g].wait()
    pl.semaphore_wait(barrier, sum(flag.astype(jnp.int32) for flag in has.values()))
    start(xs, lambda way: [x_copy(way, 0)])

    def ready(g, carry):
        prepare(g)
        start(zs, lambda way: [z_copy(way, 0, g)])
        return carry

    lax.fori_loop(0, GROUPS, ready, 0)
    start(xs, lambda way: [x_copy(way, level) for level in (1, 2)])
    start(zs, lambda way: [z_copy(way, 1, g) for g in range(GROUPS)])

    for load in loads[GROUPS:]:
        load.wait()
    lane = lax.broadcasted_iota(jnp.int32, (VARS, GROUPS * LANES), 1)
    row = lax.broadcasted_iota(jnp.int32, (VARS, GROUPS * LANES), 0)
    pick = jnp.where((lane >= row * LEVELS) & (lane < (row + 1) * LEVELS), 1.0, 0.0).astype(F32)
    col = lax.broadcasted_iota(jnp.int32, (8, LANES), 0)
    for level in range(GENS):
        for axis in range(2):
            raw = hk[level, :, axis]
            norm = raw / jnp.sum(raw, axis=-1, keepdims=True)
            spread = lax.dot_general(norm, pick, (((0,), (0,)), ((), ())),
                                     precision=lax.Precision.HIGHEST, preferred_element_type=F32)
            for g in range(GROUPS):
                for step in range(TAPS):
                    taps[level, axis, g, step] = jnp.broadcast_to(
                        spread[step:step + 1, g * LANES:(g + 1) * LANES], (8, LANES))
        for g in range(GROUPS):
            for j in range(1, 8):
                right = taps[level, 1, g, HALF + j] if j <= HALF else 0.0
                left = taps[level, 1, g, j - HALF] if j >= HALF else 0.0
                coef[level, g, j - 1] = jnp.where(col >= 8 - j, right, left)
    scale = jnp.dot(gw[...], pick, precision=lax.Precision.HIGHEST, preferred_element_type=F32)
    wfull[...] = jnp.zeros_like(wfull)
    for level in range(GENS):
        for g in range(GROUPS):
            wfull[0:LEVELS, 0:LEVELS] = vert[level, 2 * g]
            wfull[LEVELS:LANES, LEVELS:LANES] = vert[level, 2 * g + 1]
            whole = wfull[...] * scale[level:level + 1, g * LANES:(g + 1) * LANES]
            head = whole.astype(BF16)
            tail = (whole - head.astype(F32)).astype(BF16)
            for at in (0, LANES):
                mats[level, g, at:at + LANES, 0:LANES] = head
                mats[level, g, at:at + LANES, LANES:] = tail

    def along_x(block, level, g):
        ktaps = [taps[level, 0, g, step] for step in range(TAPS)]
        return line_sum([block[step:step + 8] for step in range(TAPS)], ktaps)

    def filters(level, g, n, wide, left):
        tiles = SIZES[level] // 8
        ktaps = [taps[level, 1, g, step] for step in range(TAPS)]
        for t in range(tiles):
            block = grids[level][g, pl.ds(8 * n, 16), 8 * t:8 * t + 8]
            wide[:, 8 + 8 * t:16 + 8 * t] = along_x(block, level, g)
        for t in range(tiles):
            first = 8 * t + HALF
            split_into(left, 64 * t, line_sum([wide[:, first + s:first + s + 8] for s in range(TAPS)], ktaps))

    def product(left, level, g):
        both = jnp.dot(left, mats[level, g], preferred_element_type=F32)
        total = both[:, 0:LANES] + both[:, LANES:]
        return total.reshape(total.shape[0] // 8, 8, LANES)

    def lanes(g):
        return pl.ds(pl.multiple_of(g * LANES, LANES), LANES)

    def put0(left, g, n):
        total = product(left[...], 0, g)
        for t in range(4):
            out[pl.ds(8 * n, 8), 8 * t:8 * t + 8, lanes(g)] = total[8 * t:8 * t + 8]

    def own0(g, n1, n2):
        filters(0, g, n1, wide0a, left0a)
        put0(left0a, g, n1)
        filters(0, g, n2, wide0b, left0b)

    def own0_all(n1, n2, after=None):
        def step(g, carry):
            put0(left0b, g - 1, n2)
            own0(g, n1, n2)
            if after is not None:
                after(g)
            return carry

        own0(0, n1, n2)
        if after is not None:
            after(0)
        lax.fori_loop(1, GROUPS, step, 0)
        put0(left0b, GROUPS - 1, n2)

    def forward(g):
        arrived(zs, lambda way: [z_copy(way, 0, g)])
        start(xs, lambda way: [corner_copy(way, g)])

    own0_all(1, 2)
    arrived(xs, lambda way: [x_copy(way, 0)])
    own0_all(0, 3, forward)
    arrived(xs, lambda way: [x_copy(way, level) for level in (1, 2)])

    def own12(g, carry):
        filters(1, g, 0, wide1a, left1a)
        filters(1, g, 1, wide1b, left1b)
        for n, left in enumerate((left1a, left1b)):
            total = product(left[...], 1, g)
            for t in range(2):
                part1[g, 8 * n:8 * n + 8, 8 * t:8 * t + 8] = total[8 * t:8 * t + 8]
        filters(2, g, 0, wide2, left2)
        part2[g] = product(left2[...], 2, g)
        return carry

    lax.fori_loop(0, GROUPS, own12, 0)

    first_row = (0, 32, 48)

    def edges(g, carry):
        arrived(zs, lambda way: [z_copy(way, 1, g)])
        arrived(xs, lambda way: [corner_copy(way, g)])
        for level in range(GENS):
            units = UNITS[level]
            for n in range(SIZES[level] // 8):
                block = jnp.concatenate([halo[g, at:at + 4] for at in units[2 * n:2 * n + 4]], axis=0)
                lines = along_x(block, level, g)
                at = first_row[level] + 8 * n
                twice[at:at + 8, 0:8] = lines
                twice[at:at + 8, 8:16] = lines
                added = line_sum([twice[at:at + 8, j:j + 8] for j in range(1, 8)],
                                 [coef[level, g, j - 1] for j in range(1, 8)])
                split_into(left_edge, 8 * at, added)

        def edge(level):
            at = 8 * first_row[level]
            return product(left_edge[at:at + 8 * SIZES[level]], level, g)

        low8 = lax.broadcasted_iota(jnp.int32, (8, 8, LANES), 1) < HALF
        total2 = part2[g] + edge(2)
        up2[:, pl.ds(0, 8, stride=2)] = total2
        up2[:, pl.ds(1, 8, stride=2)] = total2
        edge1 = edge(1)
        for n in range(2):
            mine = edge1[8 * n:8 * n + 8]
            for t in range(2):
                coarse = up2[4 * n:4 * n + 4, 8 * t:8 * t + 8]
                both = jnp.broadcast_to(coarse[:, None], (4, 2, 8, LANES)).reshape(8, 8, LANES)
                side = jnp.where(low8, mine, 0.0) if t == 0 else jnp.where(low8, 0.0, mine)
                total1 = part1[g, 8 * n:8 * n + 8, 8 * t:8 * t + 8] + side + both
                up1[8 * n:8 * n + 8, pl.ds(16 * t, 8, stride=2)] = total1
                up1[8 * n:8 * n + 8, pl.ds(16 * t + 1, 8, stride=2)] = total1
        edge0 = edge(0)
        for n in range(4):
            mine = edge0[8 * n:8 * n + 8]
            for t in range(4):
                coarse = up1[4 * n:4 * n + 4, 8 * t:8 * t + 8]
                total = jnp.broadcast_to(coarse[:, None], (4, 2, 8, LANES)).reshape(8, 8, LANES)
                if t == 0:
                    total = total + jnp.where(low8, mine, 0.0)
                if t == 3:
                    total = total + jnp.where(low8, 0.0, mine)
                out[8 * n:8 * n + 8, 8 * t:8 * t + 8, lanes(g)] += total
        return carry

    lax.fori_loop(0, GROUPS, edges, 0)

    groups = range(GROUPS)
    sent(xs, lambda way: [x_copy(way, level) for level in range(GENS)] + [corner_copy(way, g) for g in groups])
    sent(zs, lambda way: [z_copy(way, part, g) for part in range(2) for g in groups])


def solution(mesh):
    nx, ny = mesh.shape["gx"], mesh.shape["gy"]
    hbm = pltpu.MemorySpace.HBM

    def body(field, vertical, horiz_kernel, gen_weight):
        def f32(*shape):
            return pltpu.VMEM(shape, F32)

        def bf16(rows):
            return pltpu.VMEM((rows, 2 * LANES), BF16)

        operands = (field, vertical, jnp.transpose(horiz_kernel, (0, 2, 1, 3)), gen_weight)
        return pl.pallas_call(
            functools.partial(kernel, nx, ny),
            out_shape=jax.ShapeDtypeStruct(field.shape, F32),
            in_specs=[pl.BlockSpec(memory_space=hbm)] * 4,
            out_specs=pl.BlockSpec(memory_space=pltpu.MemorySpace.VMEM),
            scratch_shapes=[
                f32(GROUPS, 40, 32, LANES), f32(GROUPS, 24, 16, LANES), f32(GROUPS, 16, 8, LANES),
                f32(GROUPS, ABOVE - LOW, 8, LANES), f32(GROUPS, ROWS, 8, LANES),
                f32(8, 48, LANES), f32(8, 48, LANES), f32(8, 32, LANES), f32(8, 32, LANES), f32(8, 24, LANES),
                f32(*vertical.shape), f32(GENS, VARS, 2, TAPS), f32(*gen_weight.shape),
                f32(GENS, 2, GROUPS, TAPS, 8, LANES), f32(GENS, GROUPS, 7, 8, LANES),
                f32(LANES, LANES), pltpu.VMEM((GENS, GROUPS, 2 * LANES, 2 * LANES), BF16), f32(16, 32, LANES),
                bf16(256), bf16(256), bf16(128), bf16(128), bf16(64), f32(56, 16, LANES), bf16(448),
                f32(GROUPS, 16, 16, LANES), f32(GROUPS, 8, 8, LANES), f32(16, 32, LANES), f32(8, 16, LANES),
                pltpu.SemaphoreType.DMA((GROUPS + 3,)),
                pltpu.SemaphoreType.DMA((24,)),
                pltpu.SemaphoreType.DMA((24,)),
            ],
            compiler_params=pltpu.CompilerParams(
                collective_id=0, has_side_effects=True, vmem_limit_bytes=40 * 2 ** 20),
        )(*[pltpu.with_memory_space_constraint(operand, hbm) for operand in operands])

    return jax.shard_map(
        body, mesh=mesh, in_specs=(P("gx", "gy", None), P(), P(), P()),
        out_specs=P("gx", "gy", None), check_vma=False)
```

time: 89 us -> 18.5 us (0.21)
  the two profiles are of different devices: /device:TPU:400 before, /device:TPU:1 now
where the time goes in v2:
time: 18.5 us; the launch traced here: 18.3 us
  Pallas kernels  17.2 us (93%)
  local copies, waits for them, and re-layouts  1.15 us (6%)
    pallas_call x1, Pallas kernels, body(): pl.pallas_call(functools.partial(kernel, nx, ny), out_shape=jax.ShapeDtyp...  17.2 us
    unnamed x1, local copies, waits for them, and re-layouts  1.15 us

profile of v2, /device:TPU:1, one launch (start us, length us, event | category | flops | bytes accessed | tf_op | source)
XLA Modules:
  0.0 18.3 jit_solution(13337538549244979887)
XLA Ops:
  0.0 17.2 %shard_map.46 = f32[32,32,384]{2,1,0:T(8,128)S(1)} custom-call(f32[32,32,384]{2,1,0:T(8,128)} %field.1, f32[3,6,64,64]{3,2,1,0:T(8,128)} %vertical.1, f32[3,6,2,9]{3,2,1,0:T(2,128)} %bitcast.1, f32[3,6]{1,0:T(4,128)} %weight.1), custom_call_target="tpu_custom_call" | custom-call | tf_op jit(solution)/shard_map/pallas_call | solution.py:330
  17.2 1.1 %copy.6 = f32[32,32,384]{2,1,0:T(8,128)} copy(f32[32,32,384]{2,1,0:T(8,128)S(1)} %shard_map.46) | data formatting | bytes 3145728

commit v3 on v2

v3 whole, which is shorter than its diff:
```python
import functools

import jax
import jax.numpy as jnp
from jax import lax
from jax.experimental import pallas as pl
from jax.experimental.pallas import tpu as pltpu
from jax.sharding import PartitionSpec as P

GENS = 3
HALF = 4
TAPS = 9
VARS = 6
LEVELS = 64
LANES = 128
GROUPS = 3
SIZES = (32, 16, 8)
MESH = pl.DeviceIdType.MESH
F32 = jnp.float32
BF16 = jnp.bfloat16

STRIP = (0, 16, 20, 22)
FIRST, SECOND = (0, 24), (24, 28)
RING = 48
BELOW, ABOVE, MIDDLE, ROWS = 0, 12, 24, 32
UNITS = (
    ((0, 0), (1, 0), (1, 24), (1, 28), (1, 32), (1, 36), (1, 40), (1, 44), (1, 12), (0, 12)),
    ((0, 4), (1, 4), (0, 24), (0, 28), (1, 16), (0, 16)),
    ((0, 8), (1, 8), (1, 20), (0, 20)),
)


def line_sum(pieces, taps):
    total = taps[0] * pieces[0]
    for piece, tap in zip(pieces[1:], taps[1:]):
        total = total + tap * piece
    return total


def split_into(ref, at, values):
    rows = values.shape[0] * values.shape[1]
    flat = values.reshape(rows, LANES)
    head = flat.astype(BF16)
    ref[at:at + rows, 0:LANES] = head
    ref[at:at + rows, LANES:] = (flat - head.astype(F32)).astype(BF16)


def kernel(nx, ny, field, vertical, horiz, weight, out,
           grid0, grid1, grid2, x_out, x_in, z_out, z_in, halo,
           wide0a, wide0b, wide0c, wide1a, wide2, strip1, strip2,
           vert, hk, gw, scale, taps, coef, wfull, mats, pair, quad,
           left0a, left0b, left0c, left1a, left2, twice, left_edge, part1, part2, up1, up2,
           load_sem, send_sem, recv_sem, corner_ready):
    gx, gy = lax.axis_index("gx"), lax.axis_index("gy")
    grids = (grid0, grid1, grid2)

    has = {"xl": gx > 0, "xr": gx < nx - 1, "zl": gy > 0, "zr": gy < ny - 1}
    ids = {"xl": {"gx": gx - 1}, "xr": {"gx": gx + 1}, "zl": {"gy": gy - 1}, "zr": {"gy": gy + 1}}
    back = {"xl": "xr", "xr": "xl", "zl": "zr", "zr": "zl"}
    xs, zs = ("xl", "xr"), ("zl", "zr")

    first = (gx == 0) & (gy == 0)
    near = {"xl": (gx == 1) & (gy == 0), "zl": (gx == 0) & (gy == 1)}
    now = {way: has[way] & jnp.logical_not(near[way]) if way in near else has[way] for way in has}

    barrier = pltpu.get_barrier_semaphore()
    for way in has:
        @pl.when(has[way] & jnp.logical_not(first))
        def _(way=way):
            pl.semaphore_signal(barrier, inc=1, device_id=ids[way], device_id_type=MESH)

    @pl.when(first)
    def _():
        pl.semaphore_wait(barrier, 2)
        for way in ("xr", "zr"):
            pl.semaphore_signal(corner_ready, inc=1, device_id=ids[way], device_id_type=MESH)

    small = [
        pltpu.make_async_copy(src, dst, load_sem.at[GROUPS + n])
        for n, (src, dst) in enumerate(((horiz, hk), (weight, gw), (vertical, vert)))
    ]
    loads = [
        pltpu.make_async_copy(field.at[:, :, pl.ds(g * LANES, LANES)], grid0.at[g], load_sem.at[g])
        for g in range(GROUPS)
    ]
    for load in small[:2] + loads + small[2:]:
        load.start()

    for way in has:
        @pl.when(jnp.logical_not(has[way]))
        def _(way=way):
            if way in xs:
                x_in[xs.index(way)] = jnp.zeros((GROUPS, STRIP[3], 8, LANES), F32)
                at = BELOW if way == "xl" else ABOVE
                halo[:, at:at + 12] = jnp.zeros((GROUPS, 12, 8, LANES), F32)
            else:
                at = HALF if way == "zl" else 0
                z_in[:, :, at:at + HALF] = jnp.zeros((GROUPS, 52, HALF, LANES), F32)
    for wide, size in ((wide0a, 32), (wide0b, 32), (wide0c, 32), (wide1a, 16), (wide2, 8)):
        wide[:, 0:8] = jnp.zeros((8, 8, LANES), F32)
        wide[:, size + 8:] = jnp.zeros((8, 8, LANES), F32)

    def remote(way, src, dst, slot):
        return pltpu.make_async_remote_copy(
            src_ref=src, dst_ref=dst, send_sem=send_sem.at[slot], recv_sem=recv_sem.at[slot],
            device_id=ids[way], device_id_type=MESH)

    def x_copy(way, g):
        n = xs.index(way)
        return remote(way, x_out.at[n, g], x_in.at[1 - n, g], n * 3 + g)

    def z_copy(way, part, g):
        start, rows = (FIRST, SECOND)[part]
        cols = pl.ds(zs.index(way) * HALF, HALF)
        return remote(way, z_out.at[g, pl.ds(start, rows), cols], z_in.at[g, pl.ds(start, rows), cols],
                      6 + part * 6 + zs.index(way) * 3 + g)

    def corner_copy(way, g):
        here, there = (0, ABOVE) if way == "xl" else (12, BELOW)
        return remote(way, z_in.at[g, pl.ds(here, 12)], halo.at[g, pl.ds(there, 12)],
                      18 + xs.index(way) * 3 + g)

    def start(ways, make, gate=has):
        for way in ways:
            @pl.when(gate[way])
            def _(way=way):
                for copy in make(way):
                    copy.start()

    def arrived(ways, make):
        for way in ways:
            @pl.when(has[back[way]])
            def _(way=way):
                for copy in make(way):
                    copy.wait_recv()

    def sent(ways, make):
        for way in ways:
            @pl.when(has[way])
            def _(way=way):
                for copy in make(way):
                    copy.wait_send()

    lower = lax.broadcasted_iota(jnp.int32, (4, 8, LANES), 1) < HALF

    def prepare(g, carry):
        for fine, coarse, size in ((grid0, grid1, 16), (grid1, grid2, 8)):
            for r in range(size):
                pair[r, 0:2 * size] = fine[g, 2 * r] + fine[g, 2 * r + 1]
                coarse[g, r] = 0.25 * (
                    pair[r, pl.ds(0, size, stride=2)] + pair[r, pl.ds(1, size, stride=2)])
        for level, size in enumerate(SIZES):
            rows = ((0, 4), (size - 4, size)) if level == 0 else ((2, 4), (size - 4, size - 2))
            for n, (low, high) in enumerate(rows):
                x_out[n, g, STRIP[level]:STRIP[level + 1]] = grids[level][g, low:high].reshape(-1, 8, LANES)
        for level, here, there in (
                (0, 0, 0), (1, 0, 4), (2, 0, 8), (0, 28, 12), (1, 12, 16), (2, 4, 20),
                (0, 4, 24), (0, 8, 28), (0, 12, 32), (0, 16, 36), (0, 20, 40), (0, 24, 44)):
            size, rows = SIZES[level], pl.ds(here, 4)
            head, tail = grids[level][g, rows, 0:8], grids[level][g, rows, size - 8:size]
            z_out[g, there:there + 4] = jnp.where(lower, head, tail)
        for k in range(4):
            for odd in range(2):
                z_out[g, RING + k, 2 * odd:2 * odd + 2] = grid1[g, 4 + 2 * k + odd, 2:4]
                z_out[g, RING + k, 4 + 2 * odd:6 + 2 * odd] = grid1[g, 4 + 2 * k + odd, 12:14]
        return carry

    small[0].wait()
    small[1].wait()
    lane = lax.broadcasted_iota(jnp.int32, (VARS, GROUPS * LANES), 1)
    row = lax.broadcasted_iota(jnp.int32, (VARS, GROUPS * LANES), 0)
    pick = jnp.where((lane >= row * LEVELS) & (lane < (row + 1) * LEVELS), 1.0, 0.0).astype(F32)
    col = lax.broadcasted_iota(jnp.int32, (8, LANES), 0)
    for level in range(GENS):
        for axis in range(2):
            raw = hk[level, :, axis]
            norm = raw / jnp.sum(raw, axis=-1, keepdims=True)
            spread = lax.dot_general(norm, pick, (((0,), (0,)), ((), ())),
                                     precision=lax.Precision.HIGHEST, preferred_element_type=F32)
            for g in range(GROUPS):
                for step in range(TAPS):
                    taps[level, axis, g, step] = jnp.broadcast_to(
                        spread[step:step + 1, g * LANES:(g + 1) * LANES], (8, LANES))
        for g in range(GROUPS):
            for j in range(1, 8):
                right = taps[level, 1, g, HALF + j] if j <= HALF else 0.0
                left = taps[level, 1, g, j - HALF] if j >= HALF else 0.0
                coef[level, g, j - 1] = jnp.where(col >= 8 - j, right, left)
    scale[...] = jnp.dot(gw[...], pick, precision=lax.Precision.HIGHEST, preferred_element_type=F32)

    def matrices():
        small[2].wait()
        wfull[...] = jnp.zeros_like(wfull)
        for level in range(GENS):
            for g in range(GROUPS):
                wfull[0:LEVELS, 0:LEVELS] = vert[level, 2 * g]
                wfull[LEVELS:LANES, LEVELS:LANES] = vert[level, 2 * g + 1]
                whole = wfull[...] * scale[level:level + 1, g * LANES:(g + 1) * LANES]
                head = whole.astype(BF16)
                tail = (whole - head.astype(F32)).astype(BF16)
                for at in (0, LANES):
                    mats[level, g, at:at + LANES, 0:LANES] = head
                    mats[level, g, at:at + LANES, LANES:] = tail

    for g in range(GROUPS):
        loads[g].wait()
    lax.fori_loop(0, GROUPS, prepare, 0)
    pl.when(jnp.logical_not(first))(matrices)

    @pl.when(jnp.logical_not(first))
    def _():
        pl.semaphore_wait(barrier, sum(flag.astype(jnp.int32) for flag in now.values()))

    for g in range(GROUPS):
        start(zs, lambda way: [z_copy(way, 0, g)], now)
        start(xs, lambda way: [x_copy(way, g)], now)
    start(zs, lambda way: [z_copy(way, 1, g) for g in range(GROUPS)], now)
    pl.when(first)(matrices)

    def along_x(block, level, g):
        ktaps = [taps[level, 0, g, step] for step in range(TAPS)]
        count = block.shape[0] - 2 * HALF
        return line_sum([block[step:step + count] for step in range(TAPS)], ktaps)

    def along_y(level, g, wide, left):
        ktaps = [taps[level, 1, g, step] for step in range(TAPS)]
        for t in range(SIZES[level] // 8):
            at = 8 * t + HALF
            split_into(left, 64 * t, line_sum([wide[:, at + s:at + s + 8] for s in range(TAPS)], ktaps))

    def strips(g):
        for side in range(2):
            for level, fine, size in ((1, x_in, 16), (2, strip1, 8)):
                strip, tiles = (strip1, strip2)[level - 1], size // 8
                for r in range(2):
                    own, ring = (2 + r, r) if side == 0 else (r, 2 + r)
                    for t in range(2 * tiles):
                        if level == 1:
                            both = x_in[side, g, 8 * r + t] + x_in[side, g, 8 * r + 4 + t]
                        else:
                            both = strip1[side, 2 * r, 8 * t:8 * t + 8] + strip1[side, 2 * r + 1, 8 * t:8 * t + 8]
                        pair[2 * side + r, 8 * t:8 * t + 8] = both
                    strip[side, own] = 0.25 * (
                        pair[2 * side + r, pl.ds(0, size, stride=2)] + pair[2 * side + r, pl.ds(1, size, stride=2)])
                    for t in range(tiles):
                        strip[side, ring, 8 * t:8 * t + 8] = x_in[side, g, STRIP[level] + r * tiles + t]

    def strip(side, level, g, t):
        if level == 0:
            return jnp.concatenate([x_in[side, g, pl.ds(4 * r + t, 1)] for r in range(HALF)], axis=0)
        return (strip1, strip2)[level - 1][side, :, 8 * t:8 * t + 8]

    def inner_rows(level, g, row, wide, left):
        for t in range(SIZES[level] // 8):
            wide[:, 8 + 8 * t:16 + 8 * t] = along_x(
                grids[level][g, row - HALF:row + 12, 8 * t:8 * t + 8], level, g)
        along_y(level, g, wide, left)

    def outer_rows(level, g, wide, left):
        size = SIZES[level]
        for t in range(size // 8):
            cols, to = slice(8 * t, 8 * t + 8), slice(8 + 8 * t, 16 + 8 * t)
            low, high = strip(0, level, g, t), strip(1, level, g, t)
            if level == 2:
                wide[:, to] = along_x(jnp.concatenate([low, grid2[g], high], axis=0), level, g)
            else:
                wide[0:4, to] = along_x(jnp.concatenate([low, grids[level][g, 0:8, cols]], axis=0), level, g)
                wide[4:8, to] = along_x(
                    jnp.concatenate([grids[level][g, size - 8:size, cols], high], axis=0), level, g)
        along_y(level, g, wide, left)

    def product(left, level, g):
        both = jnp.dot(left, mats[level, g], preferred_element_type=F32)
        total = both[:, 0:LANES] + both[:, LANES:]
        return total.reshape(total.shape[0] // 8, 8, LANES)

    def lanes(g):
        return pl.ds(pl.multiple_of(g * LANES, LANES), LANES)

    def put0(left, g, low, high):
        total = product(left[...], 0, g)
        for t in range(4):
            out[low:low + 4, 8 * t:8 * t + 8, lanes(g)] = total[8 * t:8 * t + 4]
            out[high:high + 4, 8 * t:8 * t + 8, lanes(g)] = total[8 * t + 4:8 * t + 8]

    def put1(left, g, low, high):
        total = product(left[...], 1, g)
        for t in range(2):
            part1[g, low:low + 4, 8 * t:8 * t + 8] = total[8 * t:8 * t + 4]
            part1[g, high:high + 4, 8 * t:8 * t + 8] = total[8 * t + 4:8 * t + 8]

    def inner_four(g):
        inner_rows(0, g, 4, wide0a, left0a)
        put0(left0a, g, 4, 8)
        inner_rows(0, g, 12, wide0b, left0b)
        put0(left0b, g, 12, 16)
        inner_rows(1, g, 4, wide1a, left1a)
        put1(left1a, g, 4, 8)
        inner_rows(0, g, 20, wide0c, left0c)

    def inner(g, carry):
        put0(left0c, g - 1, 20, 24)
        inner_four(g)
        return carry

    inner_four(0)
    lax.fori_loop(1, GROUPS, inner, 0)
    put0(left0c, GROUPS - 1, 20, 24)

    for way in near:
        @pl.when(near[way])
        def _(way=way):
            pl.semaphore_wait(corner_ready, 1)
            if way == "xl":
                copies = [x_copy(way, g) for g in range(GROUPS)]
            else:
                copies = [z_copy(way, part, g) for part in range(2) for g in range(GROUPS)]
            for copy in copies:
                copy.start()

    def derive(g):
        for k in range(2):
            rows = z_in[g, 28 + 8 * k:36 + 8 * k].reshape(4, 2, 8, LANES)
            quad[k] = (rows[:, 0] + rows[:, 1]).reshape(32, LANES)
            means = 0.25 * (quad[k, pl.ds(0, 16, stride=2)] + quad[k, pl.ds(1, 16, stride=2)])
            for r in range(4):
                at, ring, odd = MIDDLE + 4 * k + r, RING + 2 * k + r // 2, r % 2
                halo[g, at, 0:2] = means[4 * r:4 * r + 2]
                halo[g, at, 6:8] = means[4 * r + 2:4 * r + 4]
                halo[g, at, 2:4] = z_in[g, ring, 2 * odd:2 * odd + 2]
                halo[g, at, 4:6] = z_in[g, ring, 4 + 2 * odd:6 + 2 * odd]

    def forward(g):
        arrived(zs, lambda way: [z_copy(way, 0, g)])
        start(xs, lambda way: [corner_copy(way, g)])

    def forward_first(g, carry):
        forward(g)
        return carry

    @pl.when(first)
    def _():
        lax.fori_loop(0, GROUPS, forward_first, 0)

    def outer(g, carry):
        @pl.when(jnp.logical_not(first))
        def _():
            forward(g)

        arrived(xs, lambda way: [x_copy(way, g)])
        strips(g)
        outer_rows(0, g, wide0a, left0a)
        put0(left0a, g, 0, 28)
        outer_rows(1, g, wide1a, left1a)
        put1(left1a, g, 0, 12)
        outer_rows(2, g, wide2, left2)
        part2[g] = product(left2[...], 2, g)
        return carry

    lax.fori_loop(0, GROUPS, outer, 0)

    groups = range(GROUPS)
    sent(xs, lambda way: [x_copy(way, g) for g in groups] + [corner_copy(way, g) for g in groups])
    sent(zs, lambda way: [z_copy(way, part, g) for part in range(2) for g in groups])

    first_row = (0, 32, 48)

    def edge_lines(level, g, n):
        block = jnp.concatenate(
            [(z_in if near_z else halo)[g, at:at + 4] for near_z, at in UNITS[level][2 * n:2 * n + 4]], axis=0)
        lines = along_x(block, level, g)
        at = first_row[level] + 8 * n
        twice[at:at + 8, 0:8] = lines
        twice[at:at + 8, 8:16] = lines
        added = line_sum([twice[at:at + 8, j:j + 8] for j in range(1, 8)],
                         [coef[level, g, j - 1] for j in range(1, 8)])
        split_into(left_edge, 8 * at, added)

    def edge(level, g):
        at = 8 * first_row[level]
        return product(left_edge[at:at + 8 * SIZES[level]], level, g)

    low8 = lax.broadcasted_iota(jnp.int32, (8, 8, LANES), 1) < HALF

    def edges(g, carry):
        arrived(zs, lambda way: [z_copy(way, 1, g)])
        edge_lines(0, g, 1)
        edge_lines(0, g, 2)
        derive(g)
        arrived(xs, lambda way: [corner_copy(way, g)])
        edge_lines(2, g, 0)
        total2 = part2[g] + edge(2, g)
        up2[:, pl.ds(0, 8, stride=2)] = total2
        up2[:, pl.ds(1, 8, stride=2)] = total2
        edge_lines(1, g, 0)
        edge_lines(1, g, 1)
        edge1 = edge(1, g)
        for n in range(2):
            mine = edge1[8 * n:8 * n + 8]
            for t in range(2):
                coarse = up2[4 * n:4 * n + 4, 8 * t:8 * t + 8]
                both = jnp.broadcast_to(coarse[:, None], (4, 2, 8, LANES)).reshape(8, 8, LANES)
                side = jnp.where(low8, mine, 0.0) if t == 0 else jnp.where(low8, 0.0, mine)
                total1 = part1[g, 8 * n:8 * n + 8, 8 * t:8 * t + 8] + side + both
                up1[8 * n:8 * n + 8, pl.ds(16 * t, 8, stride=2)] = total1
                up1[8 * n:8 * n + 8, pl.ds(16 * t + 1, 8, stride=2)] = total1
        edge_lines(0, g, 0)
        edge_lines(0, g, 3)
        edge0 = edge(0, g)
        for n in range(4):
            mine = edge0[8 * n:8 * n + 8]
            for t in range(4):
                coarse = up1[4 * n:4 * n + 4, 8 * t:8 * t + 8]
                total = jnp.broadcast_to(coarse[:, None], (4, 2, 8, LANES)).reshape(8, 8, LANES)
                if t == 0:
                    total = total + jnp.where(low8, mine, 0.0)
                if t == 3:
                    total = total + jnp.where(low8, 0.0, mine)
                out[8 * n:8 * n + 8, 8 * t:8 * t + 8, lanes(g)] += total
        return carry

    lax.fori_loop(0, GROUPS, edges, 0)


def solution(mesh):
    nx, ny = mesh.shape["gx"], mesh.shape["gy"]
    hbm = pltpu.MemorySpace.HBM

    def body(field, vertical, horiz_kernel, gen_weight):
        def f32(*shape):
            return pltpu.VMEM(shape, F32)

        def bf16(rows):
            return pltpu.VMEM((rows, 2 * LANES), BF16)

        operands = (field, vertical, jnp.transpose(horiz_kernel, (0, 2, 1, 3)), gen_weight)
        return pl.pallas_call(
            functools.partial(kernel, nx, ny),
            out_shape=jax.ShapeDtypeStruct(field.shape, F32),
            in_specs=[pl.BlockSpec(memory_space=hbm)] * 4,
            out_specs=pl.BlockSpec(memory_space=pltpu.MemorySpace.VMEM),
            scratch_shapes=[
                f32(GROUPS, 32, 32, LANES), f32(GROUPS, 16, 16, LANES), f32(GROUPS, 8, 8, LANES),
                f32(2, GROUPS, STRIP[3], 8, LANES), f32(2, GROUPS, STRIP[3], 8, LANES),
                f32(GROUPS, 52, 8, LANES), f32(GROUPS, 52, 8, LANES), f32(GROUPS, ROWS, 8, LANES),
                f32(8, 48, LANES), f32(8, 48, LANES), f32(8, 48, LANES),
                f32(8, 32, LANES), f32(8, 24, LANES), f32(2, 4, 16, LANES), f32(2, 4, 8, LANES),
                f32(*vertical.shape), f32(GENS, VARS, 2, TAPS), f32(*gen_weight.shape),
                f32(GENS, GROUPS * LANES),
                f32(GENS, 2, GROUPS, TAPS, 8, LANES), f32(GENS, GROUPS, 7, 8, LANES),
                f32(LANES, LANES), pltpu.VMEM((GENS, GROUPS, 2 * LANES, 2 * LANES), BF16),
                f32(16, 32, LANES), f32(2, 32, LANES),
                bf16(256), bf16(256), bf16(256), bf16(128), bf16(64), f32(56, 16, LANES), bf16(448),
                f32(GROUPS, 16, 16, LANES), f32(GROUPS, 8, 8, LANES), f32(16, 32, LANES), f32(8, 16, LANES),
                pltpu.SemaphoreType.DMA((GROUPS + 3,)),
                pltpu.SemaphoreType.DMA((24,)),
                pltpu.SemaphoreType.DMA((24,)),
                pltpu.SemaphoreType.REGULAR,
            ],
            compiler_params=pltpu.CompilerParams(
                collective_id=0, has_side_effects=True, vmem_limit_bytes=40 * 2 ** 20),
        )(*[pltpu.with_memory_space_constraint(operand, hbm) for operand in operands])

    return jax.shard_map(
        body, mesh=mesh, in_specs=(P("gx", "gy", None), P(), P(), P()),
        out_specs=P("gx", "gy", None), check_vma=False)
```

time: 18.5 us -> 16.4 us (0.89)
  Pallas kernels: 17.2 us -> 15.1 us
    pallas_call x1, Pallas kernels: 17.2 us -> 15.1 us  [body(): pl.pallas_call(functools.partial(kernel, nx, ny), out_shape=jax.ShapeDtyp...]
where the time goes in v3:
time: 16.4 us; the launch traced here: 16.3 us
  Pallas kernels  15.1 us (92%)
  local copies, waits for them, and re-layouts  1.15 us (7%)
    pallas_call x1, Pallas kernels, body(): pl.pallas_call(functools.partial(kernel, nx, ny), out_shape=jax.ShapeDtyp...  15.1 us
    unnamed x1, local copies, waits for them, and re-layouts  1.15 us

profile of v3, /device:TPU:1, one launch (start us, length us, event | category | flops | bytes accessed | tf_op | source)
XLA Modules:
  0.0 16.3 jit_solution(2480778705636831217)
XLA Ops:
  0.0 15.1 %shard_map.46 = f32[32,32,384]{2,1,0:T(8,128)S(1)} custom-call(f32[32,32,384]{2,1,0:T(8,128)} %field.1, f32[3,6,64,64]{3,2,1,0:T(8,128)} %vertical.1, f32[3,6,2,9]{3,2,1,0:T(2,128)} %bitcast.1, f32[3,6]{1,0:T(4,128)} %weight.1), custom_call_target="tpu_custom_call" | custom-call | tf_op jit(solution)/shard_map/pallas_call | solution.py:437
  15.1 1.1 %copy.6 = f32[32,32,384]{2,1,0:T(8,128)} copy(f32[32,32,384]{2,1,0:T(8,128)S(1)} %shard_map.46) | data formatting | bytes 3145728

commit v4 on v3

--- a/solution.py
+++ b/solution.py
@@ -205,17 +205,15 @@
     for g in range(GROUPS):
         loads[g].wait()
     lax.fori_loop(0, GROUPS, prepare, 0)
-    pl.when(jnp.logical_not(first))(matrices)
 
     @pl.when(jnp.logical_not(first))
     def _():
         pl.semaphore_wait(barrier, sum(flag.astype(jnp.int32) for flag in now.values()))
 
-    for g in range(GROUPS):
-        start(zs, lambda way: [z_copy(way, 0, g)], now)
-        start(xs, lambda way: [x_copy(way, g)], now)
+    start(zs, lambda way: [z_copy(way, 0, g) for g in range(GROUPS)], now)
+    start(xs, lambda way: [x_copy(way, g) for g in range(GROUPS)], now)
     start(zs, lambda way: [z_copy(way, 1, g) for g in range(GROUPS)], now)
-    pl.when(first)(matrices)
+    matrices()
 
     def along_x(block, level, g):
         ktaps = [taps[level, 0, g, step] for step in range(TAPS)]

time: 16.4 us -> 16.4 us (level)
  no operation moved by 1% of the time
where the time goes in v4:
time: 16.4 us; the launch traced here: 16.2 us
  Pallas kernels  15.1 us (92%)
  local copies, waits for them, and re-layouts  1.15 us (7%)
    pallas_call x1, Pallas kernels, body(): pl.pallas_call(functools.partial(kernel, nx, ny), out_shape=jax.ShapeDtyp...  15.1 us
    unnamed x1, local copies, waits for them, and re-layouts  1.15 us

profile of v4, /device:TPU:1, one launch (start us, length us, event | category | flops | bytes accessed | tf_op | source)
XLA Modules:
  0.0 16.2 jit_solution(5805902561307547045)
XLA Ops:
  0.0 15.1 %shard_map.46 = f32[32,32,384]{2,1,0:T(8,128)S(1)} custom-call(f32[32,32,384]{2,1,0:T(8,128)} %field.1, f32[3,6,64,64]{3,2,1,0:T(8,128)} %vertical.1, f32[3,6,2,9]{3,2,1,0:T(2,128)} %bitcast.1, f32[3,6]{1,0:T(4,128)} %weight.1), custom_call_target="tpu_custom_call" | custom-call | tf_op jit(solution)/shard_map/pallas_call | solution.py:435
  15.1 1.1 %copy.6 = f32[32,32,384]{2,1,0:T(8,128)} copy(f32[32,32,384]{2,1,0:T(8,128)S(1)} %shard_map.46) | data formatting | bytes 3145728

commit v5 on v4

--- a/solution.py
+++ b/solution.py
@@ -341,10 +341,6 @@
         lax.fori_loop(0, GROUPS, forward_first, 0)
 
     def outer(g, carry):
-        @pl.when(jnp.logical_not(first))
-        def _():
-            forward(g)
-
         arrived(xs, lambda way: [x_copy(way, g)])
         strips(g)
         outer_rows(0, g, wide0a, left0a)
@@ -355,7 +351,18 @@
         part2[g] = product(left2[...], 2, g)
         return carry
 
-    lax.fori_loop(0, GROUPS, outer, 0)
+    def forward_then_outer(g, carry):
+        @pl.when(jnp.logical_not(first) & (g < GROUPS))
+        def _():
+            forward(jnp.minimum(g, GROUPS - 1))
+
+        return outer(g - 1, carry)
+
+    @pl.when(jnp.logical_not(first))
+    def _():
+        forward(0)
+
+    lax.fori_loop(1, GROUPS + 1, forward_then_outer, 0)
 
     groups = range(GROUPS)
     sent(xs, lambda way: [x_copy(way, g) for g in groups] + [corner_copy(way, g) for g in groups])
@@ -363,14 +370,14 @@
 
     first_row = (0, 32, 48)
 
-    def edge_lines(level, g, n):
+    def edge_lines(level, g, unit):
         block = jnp.concatenate(
-            [(z_in if near_z else halo)[g, at:at + 4] for near_z, at in UNITS[level][2 * n:2 * n + 4]], axis=0)
+            [(z_in if near_z else halo)[g, at:at + 4] for near_z, at in UNITS[level][unit:unit + 3]], axis=0)
         lines = along_x(block, level, g)
-        at = first_row[level] + 8 * n
-        twice[at:at + 8, 0:8] = lines
-        twice[at:at + 8, 8:16] = lines
-        added = line_sum([twice[at:at + 8, j:j + 8] for j in range(1, 8)],
+        at = first_row[level] + 4 * unit
+        twice[at:at + 4, 0:8] = lines
+        twice[at:at + 4, 8:16] = lines
+        added = line_sum([twice[at:at + 4, j:j + 8] for j in range(1, 8)],
                          [coef[level, g, j - 1] for j in range(1, 8)])
         split_into(left_edge, 8 * at, added)
 
@@ -382,16 +389,19 @@
 
     def edges(g, carry):
         arrived(zs, lambda way: [z_copy(way, 1, g)])
-        edge_lines(0, g, 1)
-        edge_lines(0, g, 2)
+        for unit in range(1, 7):
+            edge_lines(0, g, unit)
         derive(g)
+        edge_lines(1, g, 1)
+        edge_lines(1, g, 2)
         arrived(xs, lambda way: [corner_copy(way, g)])
         edge_lines(2, g, 0)
+        edge_lines(2, g, 1)
         total2 = part2[g] + edge(2, g)
         up2[:, pl.ds(0, 8, stride=2)] = total2
         up2[:, pl.ds(1, 8, stride=2)] = total2
         edge_lines(1, g, 0)
-        edge_lines(1, g, 1)
+        edge_lines(1, g, 3)
         edge1 = edge(1, g)
         for n in range(2):
             mine = edge1[8 * n:8 * n + 8]
@@ -403,7 +413,7 @@
                 up1[8 * n:8 * n + 8, pl.ds(16 * t, 8, stride=2)] = total1
                 up1[8 * n:8 * n + 8, pl.ds(16 * t + 1, 8, stride=2)] = total1
         edge_lines(0, g, 0)
-        edge_lines(0, g, 3)
+        edge_lines(0, g, 7)
         edge0 = edge(0, g)
         for n in range(4):
             mine = edge0[8 * n:8 * n + 8]

time: 16.4 us -> 16.4 us (level)
  no operation moved by 1% of the time
where the time goes in v5:
time: 16.4 us; the launch traced here: 16.2 us
  Pallas kernels  15 us (91%)
  local copies, waits for them, and re-layouts  1.15 us (7%)
    pallas_call x1, Pallas kernels, body(): pl.pallas_call(functools.partial(kernel, nx, ny), out_shape=jax.ShapeDtyp...  15 us
    unnamed x1, local copies, waits for them, and re-layouts  1.15 us

profile of v5, /device:TPU:1, one launch (start us, length us, event | category | flops | bytes accessed | tf_op | source)
XLA Modules:
  0.0 16.2 jit_solution(9510583334551869225)
XLA Ops:
  0.0 15.0 %shard_map.46 = f32[32,32,384]{2,1,0:T(8,128)S(1)} custom-call(f32[32,32,384]{2,1,0:T(8,128)} %field.1, f32[3,6,64,64]{3,2,1,0:T(8,128)} %vertical.1, f32[3,6,2,9]{3,2,1,0:T(2,128)} %bitcast.1, f32[3,6]{1,0:T(4,128)} %weight.1), custom_call_target="tpu_custom_call" | custom-call | tf_op jit(solution)/shard_map/pallas_call | solution.py:445
  15.0 1.1 %copy.6 = f32[32,32,384]{2,1,0:T(8,128)} copy(f32[32,32,384]{2,1,0:T(8,128)S(1)} %shard_map.46) | data formatting | bytes 3145728

commit v6 on v5

--- a/solution.py
+++ b/solution.py
@@ -212,7 +212,6 @@
 
     start(zs, lambda way: [z_copy(way, 0, g) for g in range(GROUPS)], now)
     start(xs, lambda way: [x_copy(way, g) for g in range(GROUPS)], now)
-    start(zs, lambda way: [z_copy(way, 1, g) for g in range(GROUPS)], now)
     matrices()
 
     def along_x(block, level, g):
@@ -302,6 +301,7 @@
         return carry
 
     inner_four(0)
+    start(zs, lambda way: [z_copy(way, 1, g) for g in range(GROUPS)], now)
     lax.fori_loop(1, GROUPS, inner, 0)
     put0(left0c, GROUPS - 1, 20, 24)
 

time: 16.4 us -> 16.4 us (level)
  no operation moved by 1% of the time
where the time goes in v6:
time: 16.4 us; the launch traced here: 16.1 us
  Pallas kernels  15 us (91%)
  local copies, waits for them, and re-layouts  1.15 us (7%)
    pallas_call x1, Pallas kernels, body(): pl.pallas_call(functools.partial(kernel, nx, ny), out_shape=jax.ShapeDtyp...  15 us
    unnamed x1, local copies, waits for them, and re-layouts  1.15 us

profile of v6, /device:TPU:1, one launch (start us, length us, event | category | flops | bytes accessed | tf_op | source)
XLA Modules:
  0.0 16.1 jit_solution(15016229554391211080)
XLA Ops:
  0.0 15.0 %shard_map.46 = f32[32,32,384]{2,1,0:T(8,128)S(1)} custom-call(f32[32,32,384]{2,1,0:T(8,128)} %field.1, f32[3,6,64,64]{3,2,1,0:T(8,128)} %vertical.1, f32[3,6,2,9]{3,2,1,0:T(2,128)} %bitcast.1, f32[3,6]{1,0:T(4,128)} %weight.1), custom_call_target="tpu_custom_call" | custom-call | tf_op jit(solution)/shard_map/pallas_call | solution.py:445
  15.0 1.1 %copy.6 = f32[32,32,384]{2,1,0:T(8,128)} copy(f32[32,32,384]{2,1,0:T(8,128)S(1)} %shard_map.46) | data formatting | bytes 3145728
